TPU v7x, 32 devices: a whole 2x2x4 slice. The times are simulated.
32 devices in a mesh: dp: 16 (over z, y, x), tensor: 2 (over core).
Axes of the slice: x: 2, y: 2, z: 4, core: 2. Of those that a mesh axis runs over, the one named last changes fastest.
Arguments:
- queries: bfloat16 [12288, 8192], P('dp', 'tensor'), may hold values from -170 to 170
- key_value_pairs: bfloat16 [12288, 2, 1024], P('dp', None, 'tensor'), may hold values from -6 to 6
- document_numbers: int32 [12288], P('dp'), may hold values from 0 to 11, as said below
- destinations: int32 [16, 12], P('dp'), may hold values from 0 to 15, as said below
- adapter_down_weight: bfloat16 [8192, 64], P('tensor'), may hold values from -0.0625 to 0.0625
- adapter_up_weight: bfloat16 [64, 5120], P(None, 'tensor'), may hold values from -0.75 to 0.75
- cotangent: bfloat16 [12288, 5120], P('dp', 'tensor'), may hold values from -6 to 6
Outputs:
- arrived_out: bfloat16 [4096, 8192], P('dp', 'tensor')
- adapter_output: bfloat16 [12288, 5120], P('dp', 'tensor')
- grad_down: float32 [8192, 64], P('tensor')
- grad_up: float32 [64, 5120], P(None, 'tensor')
Inputs may be any that keep to these rules, and one draw needn't show every extreme that they name: `document_numbers`: within each replica's 768 rows the ids never fall and rise by one from 0 to 11: every document holds one or more consecutive rows. destinations[r, j] is the replica that takes document j of replica r. For each k from 1 to 4, exactly one document of every replica r goes to replica r XOR (16 / 2**k) (bitwise exclusive or); the other 8 stay (destination r). A document that leaves holds at most 64 rows, and every replica sends one of exactly 64 rows.
All inputs are finite; a program needn't handle non-finite values.
Results may differ from a plain program's by a relative error of at most 0.0062.
Values may be sent and summed in bfloat16 or wider, within the bound.
A program may use at most 64 MiB of HBM per device.

v0:
```python
import math

import jax
import jax.numpy as jnp
from jax import lax
from jax.sharding import PartitionSpec as P

HEAD_SIZE = 128
NDOC = 12
MOVES = 4
CAP = 64


ADAPTER_SCALE = 2.0
MASKED_SCORE = -1e30


def from_partner(value, axis, apart):
    mask = 2**apart
    pairs = [(source, source ^ mask) for source in range(lax.axis_size(axis))]
    return lax.ppermute(value, axis, pairs)


def attend_head(query_head, key_head, value_head, allowed):
    scores = lax.dot_general(
        query_head, key_head, (((1,), (1,)), ((), ())), preferred_element_type=jnp.float32
    ) * HEAD_SIZE ** (-0.5)
    scores = jnp.where(allowed, scores, MASKED_SCORE)
    row_max = jnp.max(scores, axis=1, keepdims=True)
    weights = jnp.where(allowed, jnp.exp(scores - row_max), 0.0)
    probabilities = (weights / jnp.sum(weights, axis=1, keepdims=True)).astype(jnp.bfloat16)
    return jnp.dot(probabilities, value_head, preferred_element_type=jnp.float32).astype(
        jnp.bfloat16
    )


def local_attention(query_rows, paired_rows, allowed):
    row_count = query_rows.shape[0]
    query_heads = query_rows.shape[1] // HEAD_SIZE
    kv_heads = paired_rows.shape[2] // HEAD_SIZE
    query_group_size = query_heads // kv_heads
    query_split = query_rows.reshape(row_count, query_heads, HEAD_SIZE).transpose(1, 0, 2)
    key_split = paired_rows[:, 0].reshape(row_count, kv_heads, HEAD_SIZE).transpose(1, 0, 2)
    value_split = paired_rows[:, 1].reshape(row_count, kv_heads, HEAD_SIZE).transpose(1, 0, 2)

    def one_head(head_index):
        return attend_head(
            query_split[head_index],
            key_split[head_index // query_group_size],
            value_split[head_index // query_group_size],
            allowed,
        )

    head_outputs = lax.map(one_head, jnp.arange(query_heads))
    return head_outputs.transpose(1, 0, 2).reshape(row_count, query_heads * HEAD_SIZE)


def row_products(left, right):
    return lax.dot_general(
        left, right, (((0,), (0,)), ((), ())), preferred_element_type=jnp.float32
    )


def on_device(
    queries,
    key_value_pairs,
    document_numbers,
    destinations,
    adapter_down_weight,
    adapter_up_weight,
    cotangent,
):
    token_rows = queries.shape[0]
    replica_list = lax.axis_size("dp")
    own_index = lax.axis_index("dp")
    top_bit = replica_list.bit_length() - 1
    gradient_scale = ADAPTER_SCALE / math.sqrt(token_rows * replica_list)
    partial_feedback = lax.dot_general(
        cotangent, adapter_up_weight, (((1,), (1,)), ((), ())), preferred_element_type=jnp.float32
    )
    feedback_signal = lax.psum(partial_feedback, "tensor").astype(jnp.bfloat16)
    position = jnp.arange(token_rows, dtype=jnp.int32)
    doc_ids = jnp.arange(NDOC, dtype=jnp.int32)
    member = document_numbers[:, None] == doc_ids[None, :]
    lengths = jnp.sum(member.astype(jnp.int32), axis=0)
    starts = jnp.sum((document_numbers[:, None] < doc_ids[None, :]).astype(jnp.int32), axis=0)
    offsets = jnp.arange(CAP, dtype=jnp.int32)
    targets = []
    counts = []
    for slot_index in range(MOVES):
        partner = jnp.bitwise_xor(own_index, replica_list >> slot_index + 1)
        picked = jnp.sum(jnp.where(destinations[0] == partner, doc_ids, 0))
        live_rows = offsets < lengths[picked]
        targets.append(jnp.where(live_rows, starts[picked] + offsets, token_rows))
        counts.append(lengths[picked])
    allowed = (document_numbers[:, None] == document_numbers[None, :]) & (
        position[:, None] >= position[None, :]
    )
    attention_layer = local_attention(queries, key_value_pairs, allowed)
    arrived = []
    for slot_index in range(MOVES):
        outgoing = jnp.take(attention_layer, targets[slot_index], axis=0, mode="fill", fill_value=0)
        arrived.append(from_partner(outgoing, "dp", top_bit - 1 - slot_index))
    arrived_out = jnp.concatenate(arrived, axis=0)
    adapter_hidden_part = jnp.dot(
        attention_layer, adapter_down_weight, preferred_element_type=jnp.float32
    )
    grad_down_part = row_products(attention_layer, feedback_signal)
    adapter_hidden = lax.psum(adapter_hidden_part, "tensor").astype(jnp.bfloat16)
    adapter_output = (
        ADAPTER_SCALE
        * jnp.dot(adapter_hidden, adapter_up_weight, preferred_element_type=jnp.float32)
    ).astype(jnp.bfloat16)
    grad_up_part = row_products(adapter_hidden, cotangent)
    grad_down, grad_up = lax.psum(
        (gradient_scale * grad_down_part, gradient_scale * grad_up_part), "dp"
    )
    return (arrived_out, adapter_output, grad_down, grad_up)


def solution(mesh):
    placed = (
        P("dp", "tensor"),
        P("dp", None, "tensor"),
        P("dp"),
        P("dp", None),
        P("tensor", None),
        P(None, "tensor"),
        P("dp", "tensor"),
    )
    return jax.shard_map(
        on_device,
        mesh=mesh,
        in_specs=placed,
        out_specs=(P("dp", "tensor"), P("dp", "tensor"), P("tensor", None), P(None, "tensor")),
        check_vma=False,
    )
```

profile of v0, /device:TPU:0, one launch (start us, length us, event | category | flops | bytes accessed | tf_op | source)
XLA Modules:
  0.0 524.3 jit_solution(17094590815410867868)
XLA Ops:
  13.9 8.8 %copy.19 = bf16[768,4096]{0,1:T(8,128)(2,1)} copy(bf16[768,4096]{1,0:T(8,128)(2,1)} %param.11) | data formatting | bytes 12582912 | tf_op args[0]
  22.7 3.4 fusion.29
  26.1 3.5 copy.29
  29.6 2.9 copy.30
  32.6 293.5 %while.13 = (s32[]{:T(128)}, bf16[32,768,128]{2,1,0:T(8,128)(2,1)}, s32[32]{0:T(128)S(1)}, bf16[32,768,128]{1,2,0:T(8,128)(2,1)}, bf16[4,768,128]{1,2,0:T(8,128)...) while((s32[]{:T(128)}, bf16[32,768,128]{2,1,0:T(8,128)(2,1)}, ...), condition=%wide.region_3.4_spmd.clone, body=%wide.region_0.3_spmd.clone.sunk | while | flops 315652608 | bytes 7901562 | solution.py:54
  66.7 2.6 fusion.51
  85.1 2.6 fusion.51
  130.9 2.6 fusion.51
  158.5 2.6 fusion.51
  167.6 2.6 fusion.51
  176.8 2.6 fusion.51
  186.0 2.6 fusion.51
  213.5 2.6 fusion.51
  222.7 2.6 fusion.51
  241.0 2.6 fusion.51
  250.2 2.6 fusion.51
  259.4 2.6 fusion.51
  323.5 2.6 fusion.51
  326.1 6.4 %copy_bitcast_fusion = bf16[768,4096]{1,0:T(8,128)(2,1)} fusion(bf16[32,768,128]{2,1,0:T(8,128)(2,1)} %get-tuple-element.95), kind=kLoop, calls=%fused_computation.29 | loop fusion | bytes 12582912 | tf_op jit(solution)/shard_map/reshape | solution.py:55
  337.0 5.0 gather_fusion.3
  342.1 3.0 collective-permute-start.3
  346.4 5.0 gather_fusion.2
  354.3 5.0 gather_fusion.1
  361.1 4.8 fusion.28
  367.2 5.3 %all-reduce.6 = (bf16[768,64]{0,1:T(8,128)(2,1)S(1)}, bf16[768,64]{0,1:T(8,128)(2,1)}) all-reduce(f32[768,64]{0,1:T(8,128)S(1)} %fusion.28, f32[768,64]{0,1:T(8,128)S(1)} %fusion.32), channel_id=1, replica_groups=mesh['dp'=16,'tensor'=2] {'tensor'}, use_global_device_ids=true, to_apply=%region_10.12 | all-reduce | flops 98304 | bytes 589824 | tf_op jit(solution)/shard_map/psum | solution.py:109
  372.4 5.2 convolution_multiply_fusion
  380.5 5.0 gather_fusion
  385.6 2.7 collective-permute-start
  388.3 4.0 multiply_convert_fusion
  392.3 30.3 %collective-permute-done = bf16[64,4096]{1,0:T(8,128)(2,1)S(1)} collective-permute-done((bf16[64,4096]{1,0:T(8,128)(2,1)S(1)}, bf16[64,4096]{1,0:T(8,128)(2,1)S(1)}, u32[]{:S(2)}, u32[]{:S(2)}) %collective-permute-start) | collective-permute-done | bytes 524320 | tf_op jit(solution)/shard_map/ppermute | solution.py:21
  422.6 2.7 pad_maximum_fusion
  425.3 89.0 %all-reduce.5.cloned.1.call-done = (f32[4096,64]{0,1:T(8,128)}, f32[64,2560]{1,0:T(8,128)}) async-done(((f32[4096,64]{0,1:T(8,128)}, f32[64,2560]{1,0:T(8,128)}), (f32[4096,64]{0,1:T(8,128)}, f32[64,2560]{1,0:T(8,128)})) %all-reduce.5.cloned.1.call-update) | async-done | bytes 1703952 | tf_op jit(solution)/shard_map/psum | solution.py:115
  (161 shorter events, 151.9 us)
Async XLA Ops:
  7.2 353.9 %copy-start = (bf16[4096,64]{0,1:T(8,128)(2,1)S(1)}, bf16[4096,64]{0,1:T(8,128)(2,1)}, u32[]{:S(2)}) copy-start(bf16[4096,64]{0,1:T(8,128)(2,1)} %param.15) | copy-start | bytes 1572868
  7.2 507.1 %all-reduce.5.cloned.1.call-start = ((), (), s32[]{:S(2)}) async-start(), calls=%async_computation | async-start | bytes 3407872 | tf_op jit(solution)/shard_map/psum | solution.py:115
  13.9 8.8 %copy-start.3 = (bf16[768,2,512]{2,1,0:T(2,128)(2,1)S(1)}, bf16[768,2,512]{2,1,0:T(2,128)(2,1)}, u32[]{:S(2)}) copy-start(bf16[768,2,512]{2,1,0:T(2,128)(2,1)} %param.12) | copy-start | bytes 4718596
  26.1 3.5 copy-start.4
  26.1 6.4 %copy-start.7 = (s32[768]{0:T(1024)S(1)}, s32[768]{0:T(1024)}, u32[]{:S(2)}) copy-start(s32[768]{0:T(1024)} %param.13) | copy-start | bytes 9220
  342.1 50.2 %collective-permute-start.3 = (bf16[64,4096]{1,0:T(8,128)(2,1)S(1)}, bf16[64,4096]{1,0:T(8,128)(2,1)S(1)}, u32[]{:S(2)}, u32[]{:S(2)}) collective-permute-start(bf16[64,4096]{1,0:T(8,128)(2,1)S(1)} %broadcast_select_fusion), channel_id=1, source_target_pairs={{0,2},{2,0},{4,6},{6,4},{8,10},{10,8},{12,14},{14,12},{16,18},{18,... | collective-permute-start | bytes 1572872 | tf_op jit(solution)/shard_map/ppermute | solution.py:21
  351.5 40.8 %collective-permute-start.2 = (bf16[64,4096]{1,0:T(8,128)(2,1)S(1)}, bf16[64,4096]{1,0:T(8,128)(2,1)}, u32[]{:S(2)}, u32[]{:S(2)}) collective-permute-start(bf16[64,4096]{1,0:T(8,128)(2,1)S(1)} %broadcast_select_fusion.1), channel_id=1, source_target_pairs={{0,4},{2,6},{4,0},{6,2},{8,12},{10,14},{12,8},{14,10},{16,20},{18,... | collective-permute-start | bytes 1572872 | tf_op jit(solution)/shard_map/ppermute | solution.py:21
  359.4 6.5 %copy-start.1 = (bf16[768,2560]{1,0:T(8,128)(2,1)S(1)}, bf16[768,2560]{1,0:T(8,128)(2,1)}, u32[]{:S(2)}) copy-start(bf16[768,2560]{1,0:T(8,128)(2,1)} %param.17) | copy-start | bytes 11796484
  359.4 6.5 %copy-start.5 = (bf16[64,2560]{1,0:T(8,128)(2,1)S(1)}, bf16[64,2560]{1,0:T(8,128)(2,1)}, u32[]{:S(2)}) copy-start(bf16[64,2560]{1,0:T(8,128)(2,1)} %param.16) | copy-start | bytes 983044
  359.4 32.9 %collective-permute-start.1 = (bf16[64,4096]{1,0:T(8,128)(2,1)S(1)}, bf16[64,4096]{1,0:T(8,128)(2,1)}, u32[]{:S(2)}, u32[]{:S(2)}) collective-permute-start(bf16[64,4096]{1,0:T(8,128)(2,1)S(1)} %broadcast_select_fusion.2), channel_id=1, source_target_pairs={{0,8},{2,10},{4,12},{6,14},{8,0},{10,2},{12,4},{14,6},{16,24},{18,... | collective-permute-start | bytes 1572872 | tf_op jit(solution)/shard_map/ppermute | solution.py:21
  372.4 5.2 copy-start.8
  372.4 5.2 copy-start.2
  385.6 37.0 %collective-permute-start = (bf16[64,4096]{1,0:T(8,128)(2,1)S(1)}, bf16[64,4096]{1,0:T(8,128)(2,1)S(1)}, u32[]{:S(2)}, u32[]{:S(2)}) collective-permute-start(bf16[64,4096]{1,0:T(8,128)(2,1)S(1)} %broadcast_select_fusion.3), channel_id=1, source_target_pairs={{0,16},{2,18},{4,20},{6,22},{8,24},{10,26},{12,28},{14,30},{16,0},... | collective-permute-start | bytes 1572872 | tf_op jit(solution)/shard_map/ppermute | solution.py:21
  514.3 2.3 copy-start.6
Sparse Core Ops, SparseCore 0:
  379.4 134.8 all-reduce.4
where the time goes:
time: 529 us; the launch traced here: 524 us
  matrix products  149 us (28%)
  loops' own time  125 us (24%)
  waiting for transfers between devices  119 us (22%)
  local copies, waits for them, and re-layouts  67.3 us (13%)
  other arithmetic  27.7 us (5%)
  between operations  22 us (4%)
  starting transfers between devices  8.92 us (2%)
    another operation x1, loops' own time, local_attention(): head_outputs = lax.map(one_head, jnp.arange(query_heads))  125 us
    psum x1, waiting for transfers between devices, on_device(): lax.psum((gradient_scale * grad_down_part, gradient_scale * grad_up_part)...  89 us
    dot_general x32, matrix products, attend_head(): jnp.dot(probabilities, value_head, preferred_element_type=jnp.float32)  82.6 us
    dot_general x32, matrix products, attend_head(): lax.dot_general(query_head, key_head, (((1,), (1,)), ((), ())), preferred...  49.2 us
    ppermute x4, waiting for transfers between devices, from_partner(): return lax.ppermute(value, axis, pairs)  30.3 us
    gather x4, local copies, waits for them, and re-layouts, on_device(): jnp.take(attention_layer, targets[slot_index], axis=0, mode='fill', fill_...  19.9 us
    dynamic_slice x32, local copies, waits for them, and re-layouts, local_attention(): head_outputs = lax.map(one_head, jnp.arange(query_heads))  18.6 us
    unnamed x23, local copies, waits for them, and re-layouts  18.4 us
  transfers between devices with their start and end apart: 5, of which 2 were waited for; matrix products, arithmetic and copies ran while one was open for 7% of the time, Pallas kernels for 0%

commit v1 on v0

v1 whole, which is shorter than its diff:
```python
import functools
import math

import jax
import jax.numpy as jnp
from jax import lax
from jax.experimental import pallas as pl
from jax.experimental.pallas import tpu as pltpu
from jax.sharding import PartitionSpec as P

HEAD_SIZE = 128
NDOC = 12
MOVES = 4
CAP = 64
TILE = 128
HEADS_PER_DOT = 4

ADAPTER_SCALE = 2.0
MASKED_SCORE = -1e30
EXP2_SCALE = HEAD_SIZE ** (-0.5) * math.log2(math.e)


def from_partner(value, axis, apart):
    mask = 2**apart
    pairs = [(source, source ^ mask) for source in range(lax.axis_size(axis))]
    return lax.ppermute(value, axis, pairs)


def attention_kernel(
    gradient_scale, tiles_ref, query_ref, key_ref, value_ref, doc_col_ref, doc_row_ref, target_ref,
    down_ref, feedback_ref, outgoing_ref, hidden_ref, grad_ref, attention_ref,
):
    group, block = pl.program_id(0), pl.program_id(1)
    blocks = attention_ref.shape[0] // TILE
    heads = query_ref.shape[1] // HEAD_SIZE

    def attend(count):
        width = count * TILE
        start = pl.multiple_of((block + 1 - count) * TILE, TILE)
        keys = key_ref[pl.ds(start, width), :]
        values = jnp.concatenate(
            [value_ref[pl.ds(start, width), :], jnp.ones((width, HEAD_SIZE), jnp.bfloat16)], axis=1
        )
        rows = lax.broadcasted_iota(jnp.int32, (TILE, width), 0) + block * TILE
        columns = lax.broadcasted_iota(jnp.int32, (TILE, width), 1) + start
        same = doc_col_ref[...] == doc_row_ref[:, pl.ds(start, width)]
        bias = jnp.where(same & (rows >= columns), 0.0, MASKED_SCORE)
        for first in range(0, heads, HEADS_PER_DOT):
            picked = range(first, min(first + HEADS_PER_DOT, heads))
            stacked = jnp.concatenate(
                [query_ref[:, h * HEAD_SIZE : (h + 1) * HEAD_SIZE] for h in picked], axis=0
            )
            scores = lax.dot_general(
                stacked, keys, (((1,), (1,)), ((), ())), preferred_element_type=jnp.float32
            )
            scores = scores.reshape(len(picked), TILE, width) * EXP2_SCALE + bias[None]
            row_max = jnp.max(scores, axis=2, keepdims=True)
            weights = jnp.exp2(scores - row_max).astype(jnp.bfloat16)
            product = jnp.dot(
                weights.reshape(len(picked) * TILE, width), values,
                preferred_element_type=jnp.float32,
            )
            result = (product[:, :HEAD_SIZE] / product[:, HEAD_SIZE:]).astype(jnp.bfloat16)
            for at, h in enumerate(picked):
                attention_ref[
                    pl.ds(pl.multiple_of(block * TILE, TILE), TILE),
                    h * HEAD_SIZE : (h + 1) * HEAD_SIZE,
                ] = result[at * TILE : (at + 1) * TILE]

    for count in range(1, blocks + 1):
        pl.when(tiles_ref[block] == count)(functools.partial(attend, count))

    @pl.when(block == blocks - 1)
    def _():
        attention = attention_ref[...]
        moved = lax.broadcasted_iota(jnp.int32, (MOVES * CAP, attention.shape[0]), 1)
        pick = jnp.where(moved == target_ref[...], 1.0, 0.0).astype(jnp.bfloat16)
        outgoing_ref[...] = jnp.dot(
            pick, attention, preferred_element_type=jnp.float32
        ).astype(jnp.bfloat16)
        part = jnp.dot(attention, down_ref[...], preferred_element_type=jnp.float32)

        @pl.when(group == 0)
        def _():
            hidden_ref[...] = part

        @pl.when(group > 0)
        def _():
            hidden_ref[...] += part

        grad_ref[...] = gradient_scale * jnp.dot(
            feedback_ref[...], attention, preferred_element_type=jnp.float32
        )


def attend_all(
    queries, keys, values, documents, tiles, targets, down_weight, feedback, gradient_scale
):
    rows, features = queries.shape
    groups = keys.shape[1] // HEAD_SIZE
    width = features // groups
    rank = down_weight.shape[1]
    blocks = rows // TILE
    grid_spec = pltpu.PrefetchScalarGridSpec(
        num_scalar_prefetch=1,
        grid=(groups, blocks),
        in_specs=[
            pl.BlockSpec((TILE, width), lambda g, i, t: (i, g)),
            pl.BlockSpec((rows, HEAD_SIZE), lambda g, i, t: (0, g)),
            pl.BlockSpec((rows, HEAD_SIZE), lambda g, i, t: (0, g)),
            pl.BlockSpec((TILE, 1), lambda g, i, t: (i, 0)),
            pl.BlockSpec((1, rows), lambda g, i, t: (0, 0)),
            pl.BlockSpec((MOVES * CAP, 1), lambda g, i, t: (0, 0)),
            pl.BlockSpec((width, rank), lambda g, i, t: (g, 0)),
            pl.BlockSpec((rank, rows), lambda g, i, t: (0, 0)),
        ],
        out_specs=[
            pl.BlockSpec((MOVES * CAP, width), lambda g, i, t: (0, g)),
            pl.BlockSpec((rows, rank), lambda g, i, t: (0, 0)),
            pl.BlockSpec((rank, width), lambda g, i, t: (0, g)),
        ],
        scratch_shapes=[pltpu.VMEM((rows, width), jnp.bfloat16)],
    )
    return pl.pallas_call(
        functools.partial(attention_kernel, gradient_scale),
        grid_spec=grid_spec,
        out_shape=[
            jax.ShapeDtypeStruct((MOVES * CAP, features), jnp.bfloat16),
            jax.ShapeDtypeStruct((rows, rank), jnp.float32),
            jax.ShapeDtypeStruct((rank, features), jnp.float32),
        ],
        compiler_params=pltpu.CompilerParams(vmem_limit_bytes=40 * 2**20),
        cost_estimate=pl.CostEstimate(
            flops=3 * rows * rows * features, bytes_accessed=4 * rows * features,
            transcendentals=rows * rows * features // (2 * HEAD_SIZE),
        ),
    )(
        tiles, queries, keys, values, documents[:, None], documents[None, :], targets[:, None],
        down_weight, feedback,
    )


def on_device(
    queries,
    key_value_pairs,
    document_numbers,
    destinations,
    adapter_down_weight,
    adapter_up_weight,
    cotangent,
):
    token_rows = queries.shape[0]
    replica_list = lax.axis_size("dp")
    own_index = lax.axis_index("dp")
    top_bit = replica_list.bit_length() - 1
    gradient_scale = ADAPTER_SCALE / math.sqrt(token_rows * replica_list)
    partial_feedback = lax.dot_general(
        adapter_up_weight, cotangent, (((1,), (1,)), ((), ())), preferred_element_type=jnp.float32
    )
    feedback_signal = lax.psum(partial_feedback, "tensor").astype(jnp.bfloat16)

    doc_ids = jnp.arange(NDOC, dtype=jnp.int32)
    lengths = jnp.sum((document_numbers[:, None] == doc_ids).astype(jnp.int32), axis=0)
    starts = jnp.sum((document_numbers[:, None] < doc_ids).astype(jnp.int32), axis=0)
    partners = jnp.bitwise_xor(
        own_index, jnp.array([replica_list >> k + 1 for k in range(MOVES)], jnp.int32)
    )
    chosen = destinations[0][None, :] == partners[:, None]
    sent_start = jnp.sum(jnp.where(chosen, starts, 0), axis=1)
    sent_length = jnp.sum(jnp.where(chosen, lengths, 0), axis=1)
    offsets = jnp.arange(CAP, dtype=jnp.int32)[None, :]
    targets = jnp.where(
        offsets < sent_length[:, None], sent_start[:, None] + offsets, -1
    ).reshape(MOVES * CAP)
    blocks = token_rows // TILE
    first_document = document_numbers.reshape(blocks, TILE)[:, 0]
    first_row = jnp.sum(
        (document_numbers[None, :] < first_document[:, None]).astype(jnp.int32), axis=1
    )
    tiles = jnp.arange(1, blocks + 1, dtype=jnp.int32) - first_row // TILE

    outgoing, hidden_part, grad_down_part = attend_all(
        queries, key_value_pairs[:, 0], key_value_pairs[:, 1], document_numbers, tiles, targets,
        adapter_down_weight, feedback_signal, gradient_scale,
    )
    arrived = [
        from_partner(outgoing[slot * CAP : (slot + 1) * CAP], "dp", top_bit - 1 - slot)
        for slot in range(MOVES)
    ]
    arrived_out = jnp.concatenate(arrived, axis=0)
    adapter_hidden = lax.psum(hidden_part, "tensor").astype(jnp.bfloat16)
    adapter_output = (
        ADAPTER_SCALE
        * jnp.dot(adapter_hidden, adapter_up_weight, preferred_element_type=jnp.float32)
    ).astype(jnp.bfloat16)
    grad_up_part = gradient_scale * lax.dot_general(
        adapter_hidden, cotangent, (((0,), (0,)), ((), ())), preferred_element_type=jnp.float32
    )
    grad_down, grad_up = lax.psum((grad_down_part, grad_up_part), "dp")
    return (arrived_out, adapter_output, grad_down.T, grad_up)


def solution(mesh):
    placed = (
        P("dp", "tensor"),
        P("dp", None, "tensor"),
        P("dp"),
        P("dp", None),
        P("tensor", None),
        P(None, "tensor"),
        P("dp", "tensor"),
    )
    return jax.shard_map(
        on_device,
        mesh=mesh,
        in_specs=placed,
        out_specs=(P("dp", "tensor"), P("dp", "tensor"), P("tensor", None), P(None, "tensor")),
        check_vma=False,
    )
```

time: 529 us -> 222 us (0.42)
  matrix products: 149 us -> 10.3 us
  loops' own time: 125 us -> 0 us
  local copies, waits for them, and re-layouts: 67.3 us -> 16.6 us
  Pallas kernels: 0 us -> 28.6 us
  other arithmetic: 27.7 us -> 4.96 us
  waiting for transfers between devices: 119 us -> 128 us
  between operations: 22 us -> 14.1 us
    dot_general x68 -> x2, matrix products: 145 us -> 7.19 us  [the longest x1 3.79 us: on_device(): lax.dot_general(adapter_hidden, cotangent, (((0,), (0,)), ((), ())), pref...]
    another operation x1 -> x0, loops' own time: 125 us -> none  [local_attention(): head_outputs = lax.map(one_head, jnp.arange(query_heads))]
    pallas_call x0 -> x1, Pallas kernels: none -> 28.6 us  [attend_all(): pl.pallas_call(functools.partial(attention_kernel, gradient_scale), grid_...]
    gather x4 -> x0, local copies, waits for them, and re-layouts: 19.9 us -> none  [on_device(): jnp.take(attention_layer, targets[slot_index], axis=0, mode='fill', fill_...]
    dynamic_slice x33 -> x0, local copies, waits for them, and re-layouts: 19.3 us -> none  [the longest x32 18.6 us: local_attention(): head_outputs = lax.map(one_head, jnp.arange(query_heads))]
    reduce_sum x34 -> x3, other arithmetic: 19.6 us -> 2.68 us  [the longest x1 0.94 us: on_device(): jnp.sum((document_numbers[:, None] == doc_ids).astype(jnp.int32), axis=0)]
    unnamed x23 -> x17, local copies, waits for them, and re-layouts: 18.4 us -> 9.9 us
    psum x1, waiting for transfers between devices: 89 us -> 96.4 us  [on_device(): grad_down, grad_up = lax.psum((grad_down_part, grad_up_part), 'dp')]
  transfers between devices with their start and end apart: 5 -> 5, of which waited for: 2 -> 3; matrix products, arithmetic and copies ran while one was open for 7% -> 2% of each run, Pallas kernels for 0% -> 0%
where the time goes in v1:
time: 222 us
  waiting for transfers between devices  128 us (58%)
  Pallas kernels  28.6 us (13%)
  local copies, waits for them, and re-layouts  16.6 us (7%)
  between operations  14.1 us (6%)
  matrix products  10.3 us (5%)
  blocking collectives  10.1 us (5%)
  starting transfers between devices  9 us (4%)
  other arithmetic  4.96 us (2%)
    psum x1, waiting for transfers between devices, on_device(): grad_down, grad_up = lax.psum((grad_down_part, grad_up_part), 'dp')  96.4 us
    ppermute x4, waiting for transfers between devices, from_partner(): return lax.ppermute(value, axis, pairs)  31.5 us
    pallas_call x1, Pallas kernels, attend_all(): pl.pallas_call(functools.partial(attention_kernel, gradient_scale), grid_...  28.6 us
    unnamed x17, local copies, waits for them, and re-layouts  9.9 us
    ppermute x4, starting transfers between devices, from_partner(): return lax.ppermute(value, axis, pairs)  8.96 us
    psum x1, blocking collectives, on_device(): adapter_hidden = lax.psum(hidden_part, 'tensor').astype(jnp.bfloat16)  5.27 us
    psum x1, blocking collectives, on_device(): feedback_signal = lax.psum(partial_feedback, 'tensor').astype(jnp.bfloat16)  4.82 us
  transfers between devices with their start and end apart: 5, of which 3 were waited for; matrix products, arithmetic and copies ran while one was open for 2% of the time, Pallas kernels for 0%

profile of v1, /device:TPU:0, one launch (start us, length us, event | category | flops | bytes accessed | tf_op | source)
XLA Modules:
  0.0 221.6 jit_solution(6763866487232921493)
XLA Ops:
  7.2 0.9 convert_reduce_fusion.1
  8.2 0.7 broadcast_in_dim.32.doc_row_ref
  8.9 1.6 broadcast_in_dim.37.doc_col_ref
  10.5 0.8 slice_reduce_fusion
  11.3 0.9 convert_reduce_fusion.2
  12.2 0.7 broadcast_xor_fusion
  12.8 0.9 fusion.2
  13.7 0.1 add_select_fusion
  13.8 0.8 select_n.31.target_ref
  14.6 3.4 %fusion.7 = f32[64,768]{1,0:T(8,128)S(1)} fusion(bf16[64,2560]{1,0:T(8,128)(2,1)S(1)} %copy-done, bf16[768,2560]{1,0:T(8,128)(2,1)} %param.14), kind=kOutput, calls=%fused_computation.27 | convolution fusion | flops 251658240 | bytes 4456448 | tf_op jit(solution)/shard_map/dot_general | solution.py:157
  18.0 4.8 %all-reduce.6.feedback_ref = bf16[64,768]{1,0:T(8,128)(2,1)} all-reduce(f32[64,768]{1,0:T(8,128)S(1)} %fusion.7), channel_id=1, replica_groups=mesh['dp'=16,'tensor'=2] {'tensor'}, use_global_device_ids=true, to_apply=%region_5.6 | all-reduce | flops 49152 | bytes 294912 | tf_op jit(solution)/shard_map/psum | solution.py:160
  22.8 1.5 copy.29.down_ref
  24.3 2.2 %fusion.6 = (bf16[768,1,512]{2,1,0:T(2,128)(2,1)S(1)}, bf16[768,1,512]{2,1,0:T(2,128)(2,1)S(1)}) fusion(bf16[768,2,512]{2,1,0:T(2,128)(2,1)S(1)} %copy-done.6), kind=kLoop, calls=%fused_computation.26 | loop fusion | bytes 3145728 | tf_op jit(solution)/shard_map/slice | solution.py:183
  26.6 0.4 copy_bitcast_fusion
  27.1 0.5 copy-done.1
  27.7 2.8 %copy-done.5 = bf16[768,4096]{1,0:T(8,128)(2,1)S(1)} copy-done((bf16[768,4096]{1,0:T(8,128)(2,1)S(1)}, bf16[768,4096]{1,0:T(8,128)(2,1)}, u32[]{:S(2)}) %copy-start.5) | copy-done | bytes 6291480
  30.4 28.6 %shard_map.111 = (bf16[256,4096]{1,0:T(8,128)(2,1)S(1)}, f32[768,64]{1,0:T(8,128)S(1)}, f32[64,4096]{1,0:T(8,128)}) custom-call(s32[6]{0:T(128)S(1)} %fusion.4.tiles_ref, bf16[768,4096]{1,0:T(8,128)(2,1)S(1)} %copy-done.5, bf16[768,512]{1,0:T(8,128)(2,1)S(1)} %get-tuple-element.23.key_ref, bf16[768,512]{1,0:T(8,128)(2,1)S(1)} %get-tuple-element.22.value_ref, ...), custom_call_target="tpu_custom_call" | custom-call | flops 7247757312 | bytes 12582912 | tf_op jit(solution)/shard_map/pallas_call | solution.py:124
  59.1 0.7 copy-done.2
  59.8 5.3 %all-reduce.7 = bf16[768,64]{1,0:T(8,128)(2,1)S(1)} all-reduce(f32[768,64]{1,0:T(8,128)} %copy-done.2), channel_id=1, replica_groups=mesh['dp'=16,'tensor'=2] {'tensor'}, use_global_device_ids=true, to_apply=%region_6.7 | all-reduce | flops 49152 | bytes 294912 | tf_op jit(solution)/shard_map/psum | solution.py:191
  65.1 3.8 %convolution_multiply_fusion = f32[64,2560]{1,0:T(8,128)} fusion(bf16[768,2560]{1,0:T(8,128)(2,1)} %param.14, bf16[768,64]{1,0:T(8,128)(2,1)S(1)} %all-reduce.7), kind=kOutput, calls=%fused_computation.1 | convolution fusion | flops 251822080 | bytes 4685824 | tf_op jit(solution)/shard_map/dot_general | solution.py:196
  68.9 0.1 fusion.5
  69.0 2.9 %collective-permute-start = (bf16[64,4096]{1,0:T(8,128)(2,1)S(1)}, bf16[64,4096]{1,0:T(8,128)(2,1)S(1)}, u32[]{:S(2)}, u32[]{:S(2)}) collective-permute-start(bf16[64,4096]{1,0:T(8,128)(2,1)S(1)} %get-tuple-element.16), channel_id=1, source_target_pairs={{0,16},{2,18},{4,20},{6,22},{8,24},{10,26},{12,28},{14,30},{16,0},... | collective-permute-start | bytes 1572872 | tf_op jit(solution)/shard_map/ppermute | solution.py:26
  71.9 2.0 collective-permute-start.3
  73.9 1.0 collective-permute-start.2
  74.9 3.1 %collective-permute-start.1 = (bf16[64,4096]{1,0:T(8,128)(2,1)S(1)}, bf16[64,4096]{1,0:T(8,128)(2,1)S(1)}, u32[]{:S(2)}, u32[]{:S(2)}) collective-permute-start(bf16[64,4096]{1,0:T(8,128)(2,1)S(1)} %get-tuple-element.19), channel_id=1, source_target_pairs={{0,8},{2,10},{4,12},{6,14},{8,0},{10,2},{12,4},{14,6},{16,24},{18,... | collective-permute-start | bytes 1572872 | tf_op jit(solution)/shard_map/ppermute | solution.py:26
  78.0 3.1 %multiply_convert_fusion = bf16[768,2560]{1,0:T(8,128)(2,1)} fusion(bf16[64,2560]{1,0:T(8,128)(2,1)S(1)} %copy-done, bf16[768,64]{1,0:T(8,128)(2,1)S(1)} %all-reduce.7), kind=kOutput, calls=%fused_computation | convolution fusion | flops 255590400 | bytes 4358144 | tf_op jit(solution)/shard_map/dot_general | solution.py:194
  81.1 28.2 %collective-permute-done = bf16[64,4096]{1,0:T(8,128)(2,1)S(1)} collective-permute-done((bf16[64,4096]{1,0:T(8,128)(2,1)S(1)}, bf16[64,4096]{1,0:T(8,128)(2,1)S(1)}, u32[]{:S(2)}, u32[]{:S(2)}) %collective-permute-start) | collective-permute-done | bytes 524320 | tf_op jit(solution)/shard_map/ppermute | solution.py:26
  109.3 3.3 %collective-permute-done.1 = bf16[64,4096]{1,0:T(8,128)(2,1)S(1)} collective-permute-done((bf16[64,4096]{1,0:T(8,128)(2,1)S(1)}, bf16[64,4096]{1,0:T(8,128)(2,1)S(1)}, u32[]{:S(2)}, u32[]{:S(2)}) %collective-permute-start.1) | collective-permute-done | bytes 524320 | tf_op jit(solution)/shard_map/ppermute | solution.py:26
  112.6 1.5 pad_maximum_fusion
  114.1 96.4 %all-reduce.5.cloned.1.call-done = (f32[4096,64]{0,1:T(8,128)}, f32[64,2560]{1,0:T(8,128)}) async-done(((f32[4096,64]{0,1:T(8,128)}, f32[64,2560]{1,0:T(8,128)}), (f32[4096,64]{0,1:T(8,128)}, f32[64,2560]{1,0:T(8,128)})) %all-reduce.5.cloned.1.call-update) | async-done | bytes 1703952 | tf_op jit(solution)/shard_map/psum | solution.py:199
  210.5 2.3 %copy.40 = f32[4096,64]{0,1:T(8,128)} copy(f32[4096,64]{0,1:T(8,128)} %get-tuple-element.26) | data formatting | bytes 2097152
  212.8 2.0 copy.41
  (16 shorter events, 0.2 us)
Async XLA Ops:
  7.2 7.4 %copy-start = (bf16[64,2560]{1,0:T(8,128)(2,1)S(1)}, bf16[64,2560]{1,0:T(8,128)(2,1)}, u32[]{:S(2)}) copy-start(bf16[64,2560]{1,0:T(8,128)(2,1)} %param.13) | copy-start | bytes 983044
  7.2 17.1 %copy-start.6 = (bf16[768,2,512]{2,1,0:T(2,128)(2,1)S(1)}, bf16[768,2,512]{2,1,0:T(2,128)(2,1)}, u32[]{:S(2)}) copy-start(bf16[768,2,512]{2,1,0:T(2,128)(2,1)} %param.9) | copy-start | bytes 4718596
  7.2 203.4 %all-reduce.5.cloned.1.call-start = ((), (), s32[]{:S(2)}) async-start(), calls=%async_computation | async-start | bytes 3407872 | tf_op jit(solution)/shard_map/psum | solution.py:199
  26.6 1.0 copy-start.1
  26.6 1.0 copy-start.3
  26.6 1.1 copy-start.4
  27.7 2.8 %copy-start.5 = (bf16[768,4096]{1,0:T(8,128)(2,1)S(1)}, bf16[768,4096]{1,0:T(8,128)(2,1)}, u32[]{:S(2)}) copy-start(bf16[768,4096]{1,0:T(8,128)(2,1)} %query_ref.1) | copy-start | bytes 18874372
  59.1 0.7 copy-start.2
  69.0 40.2 %collective-permute-start = (bf16[64,4096]{1,0:T(8,128)(2,1)S(1)}, bf16[64,4096]{1,0:T(8,128)(2,1)S(1)}, u32[]{:S(2)}, u32[]{:S(2)}) collective-permute-start(bf16[64,4096]{1,0:T(8,128)(2,1)S(1)} %get-tuple-element.16), channel_id=1, source_target_pairs={{0,16},{2,18},{4,20},{6,22},{8,24},{10,26},{12,28},{14,30},{16,0},... | collective-permute-start | bytes 1572872 | tf_op jit(solution)/shard_map/ppermute | solution.py:26
  71.9 37.3 %collective-permute-start.3 = (bf16[64,4096]{1,0:T(8,128)(2,1)S(1)}, bf16[64,4096]{1,0:T(8,128)(2,1)S(1)}, u32[]{:S(2)}, u32[]{:S(2)}) collective-permute-start(bf16[64,4096]{1,0:T(8,128)(2,1)S(1)} %get-tuple-element.17), channel_id=1, source_target_pairs={{0,2},{2,0},{4,6},{6,4},{8,10},{10,8},{12,14},{14,12},{16,18},{18,... | collective-permute-start | bytes 1572872 | tf_op jit(solution)/shard_map/ppermute | solution.py:26
  73.9 35.3 %collective-permute-start.2 = (bf16[64,4096]{1,0:T(8,128)(2,1)S(1)}, bf16[64,4096]{1,0:T(8,128)(2,1)S(1)}, u32[]{:S(2)}, u32[]{:S(2)}) collective-permute-start(bf16[64,4096]{1,0:T(8,128)(2,1)S(1)} %get-tuple-element.18), channel_id=1, source_target_pairs={{0,4},{2,6},{4,0},{6,2},{8,12},{10,14},{12,8},{14,10},{16,20},{18,... | collective-permute-start | bytes 1572872 | tf_op jit(solution)/shard_map/ppermute | solution.py:26
  74.9 37.7 %collective-permute-start.1 = (bf16[64,4096]{1,0:T(8,128)(2,1)S(1)}, bf16[64,4096]{1,0:T(8,128)(2,1)S(1)}, u32[]{:S(2)}, u32[]{:S(2)}) collective-permute-start(bf16[64,4096]{1,0:T(8,128)(2,1)S(1)} %get-tuple-element.19), channel_id=1, source_target_pairs={{0,8},{2,10},{4,12},{6,14},{8,0},{10,2},{12,4},{14,6},{16,24},{18,... | collective-permute-start | bytes 1572872 | tf_op jit(solution)/shard_map/ppermute | solution.py:26
Sparse Core Ops, SparseCore 0:
  69.0 141.4 all-reduce.4

commit v2 on v1

--- a/solution.py
+++ b/solution.py
@@ -18,12 +18,6 @@
 ADAPTER_SCALE = 2.0
 MASKED_SCORE = -1e30
 EXP2_SCALE = HEAD_SIZE ** (-0.5) * math.log2(math.e)
-
-
-def from_partner(value, axis, apart):
-    mask = 2**apart
-    pairs = [(source, source ^ mask) for source in range(lax.axis_size(axis))]
-    return lax.ppermute(value, axis, pairs)
 
 
 def attention_kernel(
@@ -140,6 +134,240 @@
     )
 
 
+def exchange_kernel(
+    sizes, gradient_scale, outgoing_ref, hidden_ref, down_part_ref, up_ref, cotangent_ref,
+    arrived_ref, output_ref, grad_down_ref, grad_up_ref,
+    hidden_in, parts0, parts1, near0, near1, sums0, sums1, far0, far1, whole0, whole1,
+    move_send, move_recv, hidden_send, hidden_recv, near_send, near_recv, far_send, far_recv,
+    back_send, back_recv, full_send, full_recv,
+):
+    near, far, cores, lanes = sizes
+    replicas = near * far
+    own = lax.axis_index("dp")
+    core = lax.axis_index("tensor")
+    mine, level = lax.rem(own, near), own // near
+    columns_out = output_ref.shape[1]
+
+    def near_peer(step):
+        return lax.rem(mine + step, near)
+
+    def far_peer(step):
+        return lax.rem(level + step, far)
+
+    def at_near(step):
+        return {"dp": level * near + near_peer(step)}
+
+    def at_far(step):
+        return {"dp": far_peer(step) * near + mine}
+
+    def at_core(step):
+        return {"tensor": lax.rem(core + step, cores)}
+
+    devices = [at_near(d) for d in range(1, near)] + [at_far(d) for d in range(1, far)]
+    devices += [at_core(d) for d in range(1, cores)]
+    barrier = pltpu.get_barrier_semaphore()
+    for device in devices:
+        pl.semaphore_signal(barrier, inc=1, device_id=device, device_id_type=pl.DeviceIdType.MESH)
+    pl.semaphore_wait(barrier, len(devices))
+
+    started = []
+
+    def send(source, target, send_sem, recv_sem, device):
+        copy = pltpu.make_async_remote_copy(
+            src_ref=source, dst_ref=target, send_sem=send_sem, recv_sem=recv_sem,
+            device_id=device, device_id_type=pl.DeviceIdType.MESH,
+        )
+        copy.start()
+        started.append(copy)
+        return copy
+
+    hidden_copies = [
+        send(hidden_ref, hidden_in.at[d], hidden_send.at[d], hidden_recv.at[d], at_core(d))
+        for d in range(1, cores)
+    ]
+
+    def fill(parts, value):
+        width = parts.shape[3]
+        for chunk in range(replicas):
+            row, lane = chunk // lanes, chunk % lanes
+            have = max(0, min(width, value.shape[1] - lane * width))
+            slot = parts.at[chunk // far, chunk % far]
+            if have < width:
+                slot[...] = jnp.zeros((16, width), jnp.bfloat16)
+            if have:
+                slot[:, :have] = value[
+                    row * 16 : (row + 1) * 16, lane * width : lane * width + have
+                ].astype(jnp.bfloat16)
+
+    def scatter_near(at, parts, arrivals):
+        return [
+            send(
+                parts.at[near_peer(d)], arrivals.at[d], near_send.at[at, d], near_recv.at[at, d],
+                at_near(d),
+            )
+            for d in range(1, near)
+        ]
+
+    fill(parts0, down_part_ref)
+    near_copies0 = scatter_near(0, parts0, near0)
+
+    move_copies = []
+    for k in range(MOVES):
+        bit = replicas >> k + 1
+        partner = own + bit - 2 * bit * lax.rem(own // bit, 2)
+        rows = pl.ds(k * CAP, CAP)
+        move_copies.append(
+            send(
+                outgoing_ref.at[rows], arrived_ref.at[rows], move_send.at[k], move_recv.at[k],
+                {"dp": partner},
+            )
+        )
+
+    total = hidden_ref[...]
+    for d, copy in enumerate(hidden_copies):
+        copy.wait_recv()
+        total = total + hidden_in[d + 1]
+    hidden = total.astype(jnp.bfloat16)
+    hidden_turned = total.T.astype(jnp.bfloat16)
+    fill(
+        parts1,
+        gradient_scale
+        * jnp.dot(hidden_turned, cotangent_ref[...], preferred_element_type=jnp.float32),
+    )
+    near_copies1 = scatter_near(1, parts1, near1)
+
+    step = 640 if columns_out % 640 == 0 else 128
+    for first in range(0, columns_out, step):
+        output_ref[:, first : first + step] = (
+            ADAPTER_SCALE
+            * jnp.dot(
+                hidden, up_ref[:, first : first + step], preferred_element_type=jnp.float32
+            )
+        ).astype(jnp.bfloat16)
+
+    def sum_near(copies, parts, arrivals, sums):
+        value = parts[mine].astype(jnp.float32)
+        for d, copy in enumerate(copies):
+            copy.wait_recv()
+            value = value + arrivals[d + 1].astype(jnp.float32)
+        sums[...] = value.astype(jnp.bfloat16)
+
+    def scatter_far(at, sums, arrivals):
+        return [
+            send(
+                sums.at[far_peer(d)], arrivals.at[d], far_send.at[at, d], far_recv.at[at, d],
+                at_far(d),
+            )
+            for d in range(1, far)
+        ]
+
+    def sum_far(copies, sums, arrivals, whole):
+        value = sums[level].astype(jnp.float32)
+        for d, copy in enumerate(copies):
+            copy.wait_recv()
+            value = value + arrivals[d + 1].astype(jnp.float32)
+        whole[mine, level] = value.astype(jnp.bfloat16)
+
+    def gather_far(at, whole):
+        return [
+            send(
+                whole.at[mine, level], whole.at[mine, level], back_send.at[at, d],
+                back_recv.at[at, d], at_far(d),
+            )
+            for d in range(1, far)
+        ]
+
+    def gather_near(at, copies, whole):
+        for copy in copies:
+            copy.wait_recv()
+        return [
+            send(
+                whole.at[mine], whole.at[mine], full_send.at[at, d], full_recv.at[at, d],
+                at_near(d),
+            )
+            for d in range(1, near)
+        ]
+
+    def give(copies, whole, target):
+        for copy in copies:
+            copy.wait_recv()
+        width = whole.shape[3]
+        for chunk in range(replicas):
+            row, lane = chunk // lanes, chunk % lanes
+            have = max(0, min(width, target.shape[1] - lane * width))
+            if have:
+                target[row * 16 : (row + 1) * 16, lane * width : lane * width + have] = whole[
+                    chunk // far, chunk % far
+                ][:, :have].astype(jnp.float32)
+
+    sum_near(near_copies0, parts0, near0, sums0)
+    far_copies0 = scatter_far(0, sums0, far0)
+    sum_near(near_copies1, parts1, near1, sums1)
+    far_copies1 = scatter_far(1, sums1, far1)
+    sum_far(far_copies0, sums0, far0, whole0)
+    back_copies0 = gather_far(0, whole0)
+    sum_far(far_copies1, sums1, far1, whole1)
+    back_copies1 = gather_far(1, whole1)
+    full_copies0 = gather_near(0, back_copies0, whole0)
+    full_copies1 = gather_near(1, back_copies1, whole1)
+    give(full_copies0, whole0, grad_down_ref)
+    give(full_copies1, whole1, grad_up_ref)
+    for copy in move_copies:
+        copy.wait_recv()
+    for copy in started:
+        copy.wait_send()
+
+
+def exchange(outgoing, hidden_part, grad_down_part, up_weight, cotangent, gradient_scale):
+    replicas, cores = lax.axis_size("dp"), lax.axis_size("tensor")
+    near = 1 << replicas.bit_length() // 2
+    far = replicas // near
+    rank, features = grad_down_part.shape
+    columns = cotangent.shape[1]
+    lanes = replicas * 16 // rank
+    widths = [-(-size // (lanes * 128)) * 128 for size in (features, columns)]
+
+    def pieces(*lead):
+        return [pltpu.VMEM((*lead, 16, width), jnp.bfloat16) for width in widths]
+
+    def semaphores(*shape):
+        return [pltpu.SemaphoreType.DMA(shape), pltpu.SemaphoreType.DMA(shape)]
+
+    vmem = pl.BlockSpec(memory_space=pltpu.VMEM)
+    hbm = pl.BlockSpec(memory_space=pl.ANY)
+    return pl.pallas_call(
+        functools.partial(exchange_kernel, (near, far, cores, lanes), gradient_scale),
+        in_specs=[hbm, vmem, vmem, vmem, vmem],
+        out_specs=[hbm, vmem, vmem, vmem],
+        out_shape=[
+            jax.ShapeDtypeStruct(outgoing.shape, jnp.bfloat16),
+            jax.ShapeDtypeStruct(cotangent.shape, jnp.bfloat16),
+            jax.ShapeDtypeStruct((rank, features), jnp.float32),
+            jax.ShapeDtypeStruct((rank, columns), jnp.float32),
+        ],
+        scratch_shapes=[
+            pltpu.VMEM((cores, *hidden_part.shape), jnp.float32),
+            *pieces(near, far),
+            *pieces(near, far),
+            *pieces(far),
+            *pieces(far),
+            *pieces(near, far),
+            *semaphores(MOVES),
+            *semaphores(cores),
+            *semaphores(2, near),
+            *semaphores(2, far),
+            *semaphores(2, far),
+            *semaphores(2, near),
+        ],
+        compiler_params=pltpu.CompilerParams(
+            collective_id=0, has_side_effects=True, vmem_limit_bytes=48 * 2**20
+        ),
+        cost_estimate=pl.CostEstimate(
+            flops=4 * rank * cotangent.size, bytes_accessed=8 * cotangent.size, transcendentals=0
+        ),
+    )(outgoing, hidden_part, grad_down_part, up_weight, cotangent)
+
+
 def on_device(
     queries,
     key_value_pairs,
@@ -152,7 +380,6 @@
     token_rows = queries.shape[0]
     replica_list = lax.axis_size("dp")
     own_index = lax.axis_index("dp")
-    top_bit = replica_list.bit_length() - 1
     gradient_scale = ADAPTER_SCALE / math.sqrt(token_rows * replica_list)
     partial_feedback = lax.dot_general(
         adapter_up_weight, cotangent, (((1,), (1,)), ((), ())), preferred_element_type=jnp.float32
@@ -183,20 +410,9 @@
         queries, key_value_pairs[:, 0], key_value_pairs[:, 1], document_numbers, tiles, targets,
         adapter_down_weight, feedback_signal, gradient_scale,
     )
-    arrived = [
-        from_partner(outgoing[slot * CAP : (slot + 1) * CAP], "dp", top_bit - 1 - slot)
-        for slot in range(MOVES)
-    ]
-    arrived_out = jnp.concatenate(arrived, axis=0)
-    adapter_hidden = lax.psum(hidden_part, "tensor").astype(jnp.bfloat16)
-    adapter_output = (
-        ADAPTER_SCALE
-        * jnp.dot(adapter_hidden, adapter_up_weight, preferred_element_type=jnp.float32)
-    ).astype(jnp.bfloat16)
-    grad_up_part = gradient_scale * lax.dot_general(
-        adapter_hidden, cotangent, (((0,), (0,)), ((), ())), preferred_element_type=jnp.float32
-    )
-    grad_down, grad_up = lax.psum((grad_down_part, grad_up_part), "dp")
+    arrived_out, adapter_output, grad_down, grad_up = exchange(
+        outgoing, hidden_part, grad_down_part, adapter_up_weight, cotangent, gradient_scale
+    )
     return (arrived_out, adapter_output, grad_down.T, grad_up)
 
 

time: 222 us -> 110 us (0.50)
  waiting for transfers between devices: 128 us -> 0 us
  Pallas kernels: 28.6 us -> 81.1 us
  between operations: 14.1 us -> 0.77 us
  starting transfers between devices: 9 us -> 0 us
  matrix products: 10.3 us -> 3.52 us
  blocking collectives: 10.1 us -> 4.39 us
    psum x1 -> x0, waiting for transfers between devices: 96.4 us -> none  [on_device(): grad_down, grad_up = lax.psum((grad_down_part, grad_up_part), 'dp')]
    pallas_call x0 -> x1, Pallas kernels: none -> 54.2 us  [exchange(): pl.pallas_call(functools.partial(exchange_kernel, (near, far, cores, lane...]
    ppermute x4 -> x0, waiting for transfers between devices: 31.5 us -> none  [from_partner(): return lax.ppermute(value, axis, pairs)]
    ppermute x4 -> x0, starting transfers between devices: 8.96 us -> none  [from_partner(): return lax.ppermute(value, axis, pairs)]
    dot_general x2 -> x0, matrix products: 6.87 us -> none  [the longest x1 3.79 us: on_device(): lax.dot_general(adapter_hidden, cotangent, (((0,), (0,)), ((), ())), pref...]
    psum x1 -> x0, blocking collectives: 5.27 us -> none  [on_device(): adapter_hidden = lax.psum(hidden_part, 'tensor').astype(jnp.bfloat16)]
    unnamed x17, local copies, waits for them, and re-layouts: 9.9 us -> 12.2 us
  transfers between devices with their start and end apart: 5 -> 0, of which waited for: 3 -> 0; matrix products, arithmetic and copies ran while one was open for 2% -> 0% of each run, Pallas kernels for 0% -> 0%
where the time goes in v2:
time: 110 us
  Pallas kernels  81.1 us (74%)
  local copies, waits for them, and re-layouts  16.7 us (15%)
  blocking collectives  4.39 us (4%)
  matrix products  3.52 us (3%)
  other arithmetic  3.3 us (3%)
    pallas_call x1, Pallas kernels, exchange(): pl.pallas_call(functools.partial(exchange_kernel, (near, far, cores, lane...  54.2 us
    pallas_call x1, Pallas kernels, attend_all(): pl.pallas_call(functools.partial(attention_kernel, gradient_scale), grid_...  26.8 us
    unnamed x17, local copies, waits for them, and re-layouts  12.2 us
    psum x1, blocking collectives, on_device(): feedback_signal = lax.psum(partial_feedback, 'tensor').astype(jnp.bfloat16)  4.39 us
    dot_general x1, matrix products, on_device(): lax.dot_general(adapter_up_weight, cotangent, (((1,), (1,)), ((), ())), p...  3.52 us
    slice x1, local copies, waits for them, and re-layouts, on_device(): key_value_pairs[:, 1]  2.24 us

profile of v2, /device:TPU:0, one launch (start us, length us, event | category | flops | bytes accessed | tf_op | source)
XLA Modules:
  0.0 109.8 jit_solution(16321244898047252969)
XLA Ops:
  0.6 0.7 broadcast_xor_fusion
  1.3 0.8 slice_reduce_fusion
  2.1 0.9 convert_reduce_fusion.2
  3.0 0.8 convert_reduce_fusion.1
  3.8 0.9 fusion
  4.7 0.1 add_select_fusion
  4.7 0.7 broadcast_in_dim.32.doc_row_ref
  5.4 0.1 select_n.31.target_ref
  5.6 0.0 copy-start.5
  5.6 3.5 %fusion.4 = f32[64,768]{1,0:T(8,128)S(1)} fusion(bf16[64,2560]{1,0:T(8,128)(2,1)} %up_ref.1, bf16[768,2560]{1,0:T(8,128)(2,1)} %cotangent_ref.1), kind=kOutput, calls=%fused_computation.21 | convolution fusion | flops 251658240 | bytes 4456448 | tf_op jit(solution)/shard_map/dot_general | solution.py:384
  9.1 0.0 copy-start.3
  9.1 4.4 %all-reduce.1.feedback_ref = bf16[64,768]{1,0:T(8,128)(2,1)S(1)} all-reduce(f32[64,768]{1,0:T(8,128)S(1)} %fusion.4), channel_id=1, replica_groups=mesh['dp'=16,'tensor'=2] {'tensor'}, use_global_device_ids=true, to_apply=%region_5.6 | all-reduce | flops 49152 | bytes 294912 | tf_op jit(solution)/shard_map/psum | solution.py:387
  13.5 0.0 copy-done.5
  13.5 0.2 broadcast_in_dim.37.doc_col_ref
  13.7 1.5 %copy.29.down_ref = bf16[4096,64]{1,0:T(8,128)(2,1)S(1)} copy(bf16[4096,64]{0,1:T(8,128)(2,1)} %param.12) | data formatting | bytes 1048576 | tf_op args[4]
  15.2 0.0 copy-done.3
  15.3 2.2 %fusion.3 = (bf16[768,1,512]{2,1,0:T(2,128)(2,1)S(1)}, bf16[768,1,512]{2,1,0:T(2,128)(2,1)S(1)}) fusion(bf16[768,2,512]{2,1,0:T(2,128)(2,1)S(1)} %copy-done.3), kind=kLoop, calls=%fused_computation.20 | loop fusion | bytes 3145728 | tf_op jit(solution)/shard_map/slice | solution.py:410
  17.5 0.4 copy_bitcast_fusion
  18.0 0.0 copy-start.2
  18.0 2.8 %copy-done.2 = bf16[768,4096]{1,0:T(8,128)(2,1)S(1)} copy-done((bf16[768,4096]{1,0:T(8,128)(2,1)S(1)}, bf16[768,4096]{1,0:T(8,128)(2,1)}, u32[]{:S(2)}) %copy-start.2) | copy-done | bytes 6291480
  20.7 0.0 copy-start.1
  20.7 26.8 %shard_map.111 = (bf16[256,4096]{1,0:T(8,128)(2,1)S(1)}, f32[768,64]{1,0:T(8,128)S(1)}, f32[64,4096]{1,0:T(8,128)S(1)}) custom-call(s32[6]{0:T(128)S(1)} %fusion.2.tiles_ref, bf16[768,4096]{1,0:T(8,128)(2,1)S(1)} %copy-done.2, bf16[768,512]{1,0:T(8,128)(2,1)S(1)} %get-tuple-element.25.key_ref, bf16[768,512]{1,0:T(8,128)(2,1)S(1)} %get-tuple-element.24.value_ref, ...), custom_call_target="tpu_custom_call" | custom-call | flops 7247757312 | bytes 12582912 | tf_op jit(solution)/shard_map/pallas_call | solution.py:118
  47.6 0.0 copy-start
  47.6 1.3 %copy-done = bf16[256,4096]{1,0:T(8,128)(2,1)} copy-done((bf16[256,4096]{1,0:T(8,128)(2,1)}, bf16[256,4096]{1,0:T(8,128)(2,1)S(1)}, u32[]{:S(2)}) %copy-start) | copy-done | bytes 2097176
  48.9 0.0 copy-done.1
  48.9 54.2 %shard_map.112 = (bf16[256,4096]{1,0:T(8,128)(2,1)S(1)}, bf16[768,2560]{1,0:T(8,128)(2,1)}, f32[64,4096]{1,0:T(8,128)S(1)}, f32[64,2560]{1,0:T(8,128)S(1)}) custom-call(bf16[256,4096]{1,0:T(8,128)(2,1)} %copy-done, f32[768,64]{1,0:T(8,128)S(1)} %get-tuple-element.12.hidden_ref, f32[64,4096]{1,0:T(8,128)S(1)} %get-tuple-element.13.down_part_ref, ...), custom_call_target="tpu_custom_call" | custom-call | flops 503316480 | bytes 15728640 | tf_op jit(solution)/shard_map/pallas_call | solution.py:338
  103.2 0.0 copy-start.4
  103.2 1.3 %copy.40 = bf16[256,4096]{1,0:T(8,128)(2,1)} copy(bf16[256,4096]{1,0:T(8,128)(2,1)S(1)} %get-tuple-element.30) | data formatting | bytes 4194304
  104.5 1.5 %copy-done.4 = bf16[768,2560]{1,0:T(8,128)(2,1)S(1)} copy-done((bf16[768,2560]{1,0:T(8,128)(2,1)S(1)}, bf16[768,2560]{1,0:T(8,128)(2,1)}, u32[]{:S(2)}) %copy-start.4) | copy-done | bytes 3932184
  106.0 1.9 %copy.41 = bf16[768,2560]{1,0:T(8,128)(2,1)} copy(bf16[768,2560]{1,0:T(8,128)(2,1)S(1)} %copy-done.4) | data formatting | bytes 7864320
  107.9 1.0 copy.42
  108.9 0.8 copy.43
  (1 shorter events, 0.0 us)
Async XLA Ops:
  5.6 8.0 %copy-start.5 = (s32[768]{0:T(1024)S(1)}, s32[768]{0:T(1024)}, u32[]{:S(2)}) copy-start(s32[768]{0:T(1024)} %param.10) | copy-start | bytes 9220
  9.1 6.1 %copy-start.3 = (bf16[768,2,512]{2,1,0:T(2,128)(2,1)S(1)}, bf16[768,2,512]{2,1,0:T(2,128)(2,1)}, u32[]{:S(2)}) copy-start(bf16[768,2,512]{2,1,0:T(2,128)(2,1)} %param.9) | copy-start | bytes 4718596
  18.0 2.8 %copy-start.2 = (bf16[768,4096]{1,0:T(8,128)(2,1)S(1)}, bf16[768,4096]{1,0:T(8,128)(2,1)}, u32[]{:S(2)}) copy-start(bf16[768,4096]{1,0:T(8,128)(2,1)} %query_ref.1) | copy-start | bytes 18874372
  20.7 28.2 %copy-start.1 = (bf16[64,2560]{1,0:T(8,128)(2,1)S(1)}, bf16[64,2560]{1,0:T(8,128)(2,1)}, u32[]{:S(2)}) copy-start(bf16[64,2560]{1,0:T(8,128)(2,1)} %up_ref.1) | copy-start | bytes 983044
  47.6 1.3 %copy-start = (bf16[256,4096]{1,0:T(8,128)(2,1)}, bf16[256,4096]{1,0:T(8,128)(2,1)S(1)}, u32[]{:S(2)}) copy-start(bf16[256,4096]{1,0:T(8,128)(2,1)S(1)} %get-tuple-element.11.outgoing_ref) | copy-start | bytes 6291460
  103.2 2.9 %copy-start.4 = (bf16[768,2560]{1,0:T(8,128)(2,1)S(1)}, bf16[768,2560]{1,0:T(8,128)(2,1)}, u32[]{:S(2)}) copy-start(bf16[768,2560]{1,0:T(8,128)(2,1)} %get-tuple-element.31) | copy-start | bytes 11796484

commit v3 on v2

--- a/solution.py
+++ b/solution.py
@@ -72,7 +72,9 @@
         outgoing_ref[...] = jnp.dot(
             pick, attention, preferred_element_type=jnp.float32
         ).astype(jnp.bfloat16)
-        part = jnp.dot(attention, down_ref[...], preferred_element_type=jnp.float32)
+        part = lax.dot_general(
+            attention, down_ref[...], (((1,), (1,)), ((), ())), preferred_element_type=jnp.float32
+        )
 
         @pl.when(group == 0)
         def _():
@@ -105,7 +107,7 @@
             pl.BlockSpec((TILE, 1), lambda g, i, t: (i, 0)),
             pl.BlockSpec((1, rows), lambda g, i, t: (0, 0)),
             pl.BlockSpec((MOVES * CAP, 1), lambda g, i, t: (0, 0)),
-            pl.BlockSpec((width, rank), lambda g, i, t: (g, 0)),
+            pl.BlockSpec((rank, width), lambda g, i, t: (0, g)),
             pl.BlockSpec((rank, rows), lambda g, i, t: (0, 0)),
         ],
         out_specs=[
@@ -130,7 +132,7 @@
         ),
     )(
         tiles, queries, keys, values, documents[:, None], documents[None, :], targets[:, None],
-        down_weight, feedback,
+        down_weight.T, feedback,
     )
 
 
@@ -181,6 +183,23 @@
         started.append(copy)
         return copy
 
+    def move(slots):
+        copies = []
+        for k in slots:
+            bit = replicas >> k + 1
+            partner = own + bit - 2 * bit * lax.rem(own // bit, 2)
+            rows = pl.ds(k * CAP, CAP)
+            copies.append(
+                send(
+                    outgoing_ref.at[rows], arrived_ref.at[rows], move_send.at[k], move_recv.at[k],
+                    {"dp": partner},
+                )
+            )
+        return copies
+
+    far_moves = [k for k in range(MOVES) if replicas >> k + 1 >= near]
+    near_moves = [k for k in range(MOVES) if replicas >> k + 1 < near]
+    move_copies = move(far_moves)
     hidden_copies = [
         send(hidden_ref, hidden_in.at[d], hidden_send.at[d], hidden_recv.at[d], at_core(d))
         for d in range(1, cores)
@@ -211,18 +230,6 @@
     fill(parts0, down_part_ref)
     near_copies0 = scatter_near(0, parts0, near0)
 
-    move_copies = []
-    for k in range(MOVES):
-        bit = replicas >> k + 1
-        partner = own + bit - 2 * bit * lax.rem(own // bit, 2)
-        rows = pl.ds(k * CAP, CAP)
-        move_copies.append(
-            send(
-                outgoing_ref.at[rows], arrived_ref.at[rows], move_send.at[k], move_recv.at[k],
-                {"dp": partner},
-            )
-        )
-
     total = hidden_ref[...]
     for d, copy in enumerate(hidden_copies):
         copy.wait_recv()
@@ -304,6 +311,7 @@
     far_copies0 = scatter_far(0, sums0, far0)
     sum_near(near_copies1, parts1, near1, sums1)
     far_copies1 = scatter_far(1, sums1, far1)
+    move_copies += move(near_moves)
     sum_far(far_copies0, sums0, far0, whole0)
     back_copies0 = gather_far(0, whole0)
     sum_far(far_copies1, sums1, far1, whole1)
@@ -337,7 +345,7 @@
     hbm = pl.BlockSpec(memory_space=pl.ANY)
     return pl.pallas_call(
         functools.partial(exchange_kernel, (near, far, cores, lanes), gradient_scale),
-        in_specs=[hbm, vmem, vmem, vmem, vmem],
+        in_specs=[vmem, vmem, vmem, vmem, vmem],
         out_specs=[hbm, vmem, vmem, vmem],
         out_shape=[
             jax.ShapeDtypeStruct(outgoing.shape, jnp.bfloat16),

time: 110 us -> 106 us (0.964)
  local copies, waits for them, and re-layouts: 16.7 us -> 13.1 us
    unnamed x17 -> x20, local copies, waits for them, and re-layouts: 12.2 us -> 8.62 us
where the time goes in v3:
time: 106 us
  Pallas kernels  80.7 us (76%)
  local copies, waits for them, and re-layouts  13.1 us (12%)
  blocking collectives  4.27 us (4%)
  matrix products  3.62 us (3%)
  other arithmetic  3.3 us (3%)
    pallas_call x1, Pallas kernels, exchange(): pl.pallas_call(functools.partial(exchange_kernel, (near, far, cores, lane...  53.8 us
    pallas_call x1, Pallas kernels, attend_all(): pl.pallas_call(functools.partial(attention_kernel, gradient_scale), grid_...  26.9 us
    unnamed x20, local copies, waits for them, and re-layouts  8.62 us
    psum x1, blocking collectives, on_device(): feedback_signal = lax.psum(partial_feedback, 'tensor').astype(jnp.bfloat16)  4.27 us
    dot_general x1, matrix products, on_device(): lax.dot_general(adapter_up_weight, cotangent, (((1,), (1,)), ((), ())), p...  3.62 us
    slice x1, local copies, waits for them, and re-layouts, on_device(): key_value_pairs[:, 1]  2.24 us

profile of v3, /device:TPU:0, one launch (start us, length us, event | category | flops | bytes accessed | tf_op | source)
XLA Modules:
  0.0 105.7 jit_solution(1278667943690208932)
XLA Ops:
  0.6 0.7 broadcast_xor_fusion
  1.3 0.8 slice_reduce_fusion
  2.1 0.9 convert_reduce_fusion.2
  3.0 0.8 convert_reduce_fusion.1
  3.8 0.9 fusion
  4.7 0.1 add_select_fusion
  4.7 0.7 broadcast_in_dim.32.doc_row_ref
  5.4 0.1 select_n.31.target_ref
  5.6 0.0 copy-start.5
  5.6 0.0 copy-start.3
  5.6 3.6 %fusion.4 = f32[64,768]{1,0:T(8,128)S(1)} fusion(bf16[64,2560]{1,0:T(8,128)(2,1)} %up_ref.1, bf16[768,2560]{1,0:T(8,128)(2,1)} %cotangent_ref.1), kind=kOutput, calls=%fused_computation.21 | convolution fusion | flops 251658240 | bytes 4456448 | tf_op jit(solution)/shard_map/dot_general | solution.py:392
  9.2 4.3 %all-reduce.1.feedback_ref = bf16[64,768]{1,0:T(8,128)(2,1)S(1)} all-reduce(f32[64,768]{1,0:T(8,128)S(1)} %fusion.4), channel_id=1, replica_groups=mesh['dp'=16,'tensor'=2] {'tensor'}, use_global_device_ids=true, to_apply=%region_5.6 | all-reduce | flops 49152 | bytes 294912 | tf_op jit(solution)/shard_map/psum | solution.py:395
  13.5 0.0 copy-done.5
  13.5 0.0 slice-start
  13.5 0.2 broadcast_in_dim.37.doc_col_ref
  13.7 0.0 copy-done.3
  13.7 0.0 slice-start.1
  13.7 2.2 %fusion.3 = (bf16[768,1,512]{2,1,0:T(2,128)(2,1)S(1)}, bf16[768,1,512]{2,1,0:T(2,128)(2,1)S(1)}) fusion(bf16[768,2,512]{2,1,0:T(2,128)(2,1)S(1)} %copy-done.3), kind=kLoop, calls=%fused_computation.20 | loop fusion | bytes 3145728 | tf_op jit(solution)/shard_map/slice | solution.py:418
  16.0 0.0 copy-start.2
  16.0 0.4 copy_bitcast_fusion
  16.4 0.0 slice-done
  16.4 0.0 slice-done.1
  16.5 0.7 copy-done.2
  17.1 26.9 %shard_map.111 = (bf16[256,4096]{1,0:T(8,128)(2,1)S(1)}, f32[768,64]{1,0:T(8,128)S(1)}, f32[64,4096]{1,0:T(8,128)S(1)}) custom-call(s32[6]{0:T(128)S(1)} %fusion.2.tiles_ref, bf16[768,4096]{1,0:T(8,128)(2,1)S(1)} %bitcast.12, bf16[768,512]{1,0:T(8,128)(2,1)S(1)} %get-tuple-element.25.key_ref, bf16[768,512]{1,0:T(8,128)(2,1)S(1)} %get-tuple-element.24.value_ref, ...), custom_call_target="tpu_custom_call" | custom-call | flops 7247757312 | bytes 12582912 | tf_op jit(solution)/shard_map/pallas_call | solution.py:120
  44.0 0.0 copy-start
  44.0 1.3 %copy-done = bf16[256,4096]{1,0:T(8,128)(2,1)} copy-done((bf16[256,4096]{1,0:T(8,128)(2,1)}, bf16[256,4096]{1,0:T(8,128)(2,1)S(1)}, u32[]{:S(2)}) %copy-start) | copy-done | bytes 2097176
  45.3 53.8 %shard_map.112 = (bf16[256,4096]{1,0:T(8,128)(2,1)S(1)}, bf16[768,2560]{1,0:T(8,128)(2,1)}, f32[64,4096]{1,0:T(8,128)S(1)}, f32[64,2560]{1,0:T(8,128)S(1)}) custom-call(bf16[256,4096]{1,0:T(8,128)(2,1)} %copy-done, f32[768,64]{1,0:T(8,128)S(1)} %get-tuple-element.12.hidden_ref, f32[64,4096]{1,0:T(8,128)S(1)} %get-tuple-element.13.down_part_ref, ...), custom_call_target="tpu_custom_call" | custom-call | flops 503316480 | bytes 15728640 | tf_op jit(solution)/shard_map/pallas_call | solution.py:346
  99.1 1.3 %copy.36 = bf16[256,4096]{1,0:T(8,128)(2,1)} copy(bf16[256,4096]{1,0:T(8,128)(2,1)S(1)} %get-tuple-element.30) | data formatting | bytes 4194304
  100.5 1.5 %copy-done.4 = bf16[768,2560]{1,0:T(8,128)(2,1)S(1)} copy-done((bf16[768,2560]{1,0:T(8,128)(2,1)S(1)}, bf16[768,2560]{1,0:T(8,128)(2,1)}, u32[]{:S(2)}) %copy-start.4) | copy-done | bytes 3932184
  102.0 1.9 %copy.37 = bf16[768,2560]{1,0:T(8,128)(2,1)} copy(bf16[768,2560]{1,0:T(8,128)(2,1)S(1)} %copy-done.4) | data formatting | bytes 7864320
  103.9 1.0 copy.38
  104.9 0.8 copy.39
  (5 shorter events, 0.0 us)
Async XLA Ops:
  5.6 7.9 %copy-start.5 = (s32[768]{0:T(1024)S(1)}, s32[768]{0:T(1024)}, u32[]{:S(2)}) copy-start(s32[768]{0:T(1024)} %param.10) | copy-start | bytes 9220
  5.6 8.1 %copy-start.3 = (bf16[768,2,512]{2,1,0:T(2,128)(2,1)S(1)}, bf16[768,2,512]{2,1,0:T(2,128)(2,1)}, u32[]{:S(2)}) copy-start(bf16[768,2,512]{2,1,0:T(2,128)(2,1)} %param.9) | copy-start | bytes 4718596
  13.5 2.9 %slice-start = ((s8[6291456]{0:T(1024)(128)(4,1)}), s8[4194304]{0:T(1024)(128)(4,1)S(1)}, s32[]{:S(2)}) async-start(s8[6291456]{0:T(1024)(128)(4,1)} %bitcast.11), calls=%async_computation | async-start | bytes 8388608
  13.7 2.7 %slice-start.1 = ((s8[6291456]{0:T(1024)(128)(4,1)}), s8[2097152]{0:T(1024)(128)(4,1)S(1)}, s32[]{:S(2)}) async-start(s8[6291456]{0:T(1024)(128)(4,1)} %bitcast.11), calls=%async_computation.1 | async-start | bytes 4194304
  16.0 1.2 %copy-start.2 = (bf16[4096,64]{0,1:T(8,128)(2,1)S(1)}, bf16[4096,64]{0,1:T(8,128)(2,1)}, u32[]{:S(2)}) copy-start(bf16[4096,64]{0,1:T(8,128)(2,1)} %param.12) | copy-start | bytes 1572868
  17.1 28.2 %copy-start.1 = (bf16[64,2560]{1,0:T(8,128)(2,1)S(1)}, bf16[64,2560]{1,0:T(8,128)(2,1)}, u32[]{:S(2)}) copy-start(bf16[64,2560]{1,0:T(8,128)(2,1)} %up_ref.1) | copy-start | bytes 983044
  44.0 1.3 %copy-start = (bf16[256,4096]{1,0:T(8,128)(2,1)}, bf16[256,4096]{1,0:T(8,128)(2,1)S(1)}, u32[]{:S(2)}) copy-start(bf16[256,4096]{1,0:T(8,128)(2,1)S(1)} %get-tuple-element.11.outgoing_ref) | copy-start | bytes 6291460
  99.1 2.9 %copy-start.4 = (bf16[768,2560]{1,0:T(8,128)(2,1)S(1)}, bf16[768,2560]{1,0:T(8,128)(2,1)}, u32[]{:S(2)}) copy-start(bf16[768,2560]{1,0:T(8,128)(2,1)} %get-tuple-element.31) | copy-start | bytes 11796484

commit v4 on v3

--- a/solution.py
+++ b/solution.py
@@ -13,7 +13,7 @@
 MOVES = 4
 CAP = 64
 TILE = 128
-HEADS_PER_DOT = 4
+HEADS_PER_DOT = 8
 
 ADAPTER_SCALE = 2.0
 MASKED_SCORE = -1e30

time: 106 us -> 106 us (level); the launches traced: 106 us -> 105 us
  Pallas kernels: 80.7 us -> 79.5 us
    pallas_call x1, Pallas kernels: 53.8 us -> 52 us  [exchange(): pl.pallas_call(functools.partial(exchange_kernel, (near, far, cores, lane...]
where the time goes in v4:
time: 106 us; the launch traced here: 105 us
  Pallas kernels  79.5 us (75%)
  local copies, waits for them, and re-layouts  13.1 us (12%)
  blocking collectives  4.27 us (4%)
  matrix products  3.62 us (3%)
  other arithmetic  3.3 us (3%)
    pallas_call x1, Pallas kernels, exchange(): pl.pallas_call(functools.partial(exchange_kernel, (near, far, cores, lane...  52 us
    pallas_call x1, Pallas kernels, attend_all(): pl.pallas_call(functools.partial(attention_kernel, gradient_scale), grid_...  27.5 us
    unnamed x20, local copies, waits for them, and re-layouts  8.62 us
    psum x1, blocking collectives, on_device(): feedback_signal = lax.psum(partial_feedback, 'tensor').astype(jnp.bfloat16)  4.27 us
    dot_general x1, matrix products, on_device(): lax.dot_general(adapter_up_weight, cotangent, (((1,), (1,)), ((), ())), p...  3.62 us
    slice x1, local copies, waits for them, and re-layouts, on_device(): key_value_pairs[:, 1]  2.24 us

profile of v4, /device:TPU:0, one launch (start us, length us, event | category | flops | bytes accessed | tf_op | source)
XLA Modules:
  0.0 104.6 jit_solution(5960164353403854915)
XLA Ops:
  0.6 0.7 broadcast_xor_fusion
  1.3 0.8 slice_reduce_fusion
  2.1 0.9 convert_reduce_fusion.2
  3.0 0.8 convert_reduce_fusion.1
  3.8 0.9 fusion
  4.7 0.1 add_select_fusion
  4.7 0.7 broadcast_in_dim.32.doc_row_ref
  5.4 0.1 select_n.31.target_ref
  5.6 0.0 copy-start.5
  5.6 0.0 copy-start.3
  5.6 3.6 %fusion.4 = f32[64,768]{1,0:T(8,128)S(1)} fusion(bf16[64,2560]{1,0:T(8,128)(2,1)} %up_ref.1, bf16[768,2560]{1,0:T(8,128)(2,1)} %cotangent_ref.1), kind=kOutput, calls=%fused_computation.21 | convolution fusion | flops 251658240 | bytes 4456448 | tf_op jit(solution)/shard_map/dot_general | solution.py:392
  9.2 4.3 %all-reduce.1.feedback_ref = bf16[64,768]{1,0:T(8,128)(2,1)S(1)} all-reduce(f32[64,768]{1,0:T(8,128)S(1)} %fusion.4), channel_id=1, replica_groups=mesh['dp'=16,'tensor'=2] {'tensor'}, use_global_device_ids=true, to_apply=%region_5.6 | all-reduce | flops 49152 | bytes 294912 | tf_op jit(solution)/shard_map/psum | solution.py:395
  13.5 0.0 copy-done.5
  13.5 0.0 slice-start
  13.5 0.2 broadcast_in_dim.37.doc_col_ref
  13.7 0.0 copy-done.3
  13.7 0.0 slice-start.1
  13.7 2.2 %fusion.3 = (bf16[768,1,512]{2,1,0:T(2,128)(2,1)S(1)}, bf16[768,1,512]{2,1,0:T(2,128)(2,1)S(1)}) fusion(bf16[768,2,512]{2,1,0:T(2,128)(2,1)S(1)} %copy-done.3), kind=kLoop, calls=%fused_computation.20 | loop fusion | bytes 3145728 | tf_op jit(solution)/shard_map/slice | solution.py:418
  16.0 0.0 copy-start.2
  16.0 0.4 copy_bitcast_fusion
  16.4 0.0 slice-done
  16.4 0.0 slice-done.1
  16.5 0.7 copy-done.2
  17.1 27.5 %shard_map.111 = (bf16[256,4096]{1,0:T(8,128)(2,1)S(1)}, f32[768,64]{1,0:T(8,128)S(1)}, f32[64,4096]{1,0:T(8,128)S(1)}) custom-call(s32[6]{0:T(128)S(1)} %fusion.2.tiles_ref, bf16[768,4096]{1,0:T(8,128)(2,1)S(1)} %bitcast.12, bf16[768,512]{1,0:T(8,128)(2,1)S(1)} %get-tuple-element.25.key_ref, bf16[768,512]{1,0:T(8,128)(2,1)S(1)} %get-tuple-element.24.value_ref, ...), custom_call_target="tpu_custom_call" | custom-call | flops 7247757312 | bytes 12582912 | tf_op jit(solution)/shard_map/pallas_call | solution.py:120
  44.7 0.0 copy-start
  44.7 1.3 %copy-done = bf16[256,4096]{1,0:T(8,128)(2,1)} copy-done((bf16[256,4096]{1,0:T(8,128)(2,1)}, bf16[256,4096]{1,0:T(8,128)(2,1)S(1)}, u32[]{:S(2)}) %copy-start) | copy-done | bytes 2097176
  46.0 52.0 %shard_map.112 = (bf16[256,4096]{1,0:T(8,128)(2,1)S(1)}, bf16[768,2560]{1,0:T(8,128)(2,1)}, f32[64,4096]{1,0:T(8,128)S(1)}, f32[64,2560]{1,0:T(8,128)S(1)}) custom-call(bf16[256,4096]{1,0:T(8,128)(2,1)} %copy-done, f32[768,64]{1,0:T(8,128)S(1)} %get-tuple-element.12.hidden_ref, f32[64,4096]{1,0:T(8,128)S(1)} %get-tuple-element.13.down_part_ref, ...), custom_call_target="tpu_custom_call" | custom-call | flops 503316480 | bytes 15728640 | tf_op jit(solution)/shard_map/pallas_call | solution.py:346
  98.0 1.3 %copy.36 = bf16[256,4096]{1,0:T(8,128)(2,1)} copy(bf16[256,4096]{1,0:T(8,128)(2,1)S(1)} %get-tuple-element.30) | data formatting | bytes 4194304
  99.3 1.5 %copy-done.4 = bf16[768,2560]{1,0:T(8,128)(2,1)S(1)} copy-done((bf16[768,2560]{1,0:T(8,128)(2,1)S(1)}, bf16[768,2560]{1,0:T(8,128)(2,1)}, u32[]{:S(2)}) %copy-start.4) | copy-done | bytes 3932184
  100.9 1.9 %copy.37 = bf16[768,2560]{1,0:T(8,128)(2,1)} copy(bf16[768,2560]{1,0:T(8,128)(2,1)S(1)} %copy-done.4) | data formatting | bytes 7864320
  102.8 1.0 copy.38
  103.8 0.8 copy.39
  (5 shorter events, 0.0 us)
Async XLA Ops:
  5.6 7.9 %copy-start.5 = (s32[768]{0:T(1024)S(1)}, s32[768]{0:T(1024)}, u32[]{:S(2)}) copy-start(s32[768]{0:T(1024)} %param.10) | copy-start | bytes 9220
  5.6 8.1 %copy-start.3 = (bf16[768,2,512]{2,1,0:T(2,128)(2,1)S(1)}, bf16[768,2,512]{2,1,0:T(2,128)(2,1)}, u32[]{:S(2)}) copy-start(bf16[768,2,512]{2,1,0:T(2,128)(2,1)} %param.9) | copy-start | bytes 4718596
  13.5 2.9 %slice-start = ((s8[6291456]{0:T(1024)(128)(4,1)}), s8[4194304]{0:T(1024)(128)(4,1)S(1)}, s32[]{:S(2)}) async-start(s8[6291456]{0:T(1024)(128)(4,1)} %bitcast.11), calls=%async_computation | async-start | bytes 8388608
  13.7 2.7 %slice-start.1 = ((s8[6291456]{0:T(1024)(128)(4,1)}), s8[2097152]{0:T(1024)(128)(4,1)S(1)}, s32[]{:S(2)}) async-start(s8[6291456]{0:T(1024)(128)(4,1)} %bitcast.11), calls=%async_computation.1 | async-start | bytes 4194304
  16.0 1.2 %copy-start.2 = (bf16[4096,64]{0,1:T(8,128)(2,1)S(1)}, bf16[4096,64]{0,1:T(8,128)(2,1)}, u32[]{:S(2)}) copy-start(bf16[4096,64]{0,1:T(8,128)(2,1)} %param.12) | copy-start | bytes 1572868
  17.1 28.9 %copy-start.1 = (bf16[64,2560]{1,0:T(8,128)(2,1)S(1)}, bf16[64,2560]{1,0:T(8,128)(2,1)}, u32[]{:S(2)}) copy-start(bf16[64,2560]{1,0:T(8,128)(2,1)} %up_ref.1) | copy-start | bytes 983044
  44.7 1.3 %copy-start = (bf16[256,4096]{1,0:T(8,128)(2,1)}, bf16[256,4096]{1,0:T(8,128)(2,1)S(1)}, u32[]{:S(2)}) copy-start(bf16[256,4096]{1,0:T(8,128)(2,1)S(1)} %get-tuple-element.11.outgoing_ref) | copy-start | bytes 6291460
  98.0 2.9 %copy-start.4 = (bf16[768,2560]{1,0:T(8,128)(2,1)S(1)}, bf16[768,2560]{1,0:T(8,128)(2,1)}, u32[]{:S(2)}) copy-start(bf16[768,2560]{1,0:T(8,128)(2,1)} %get-tuple-element.31) | copy-start | bytes 11796484
